TPU v7x, 32 devices: a whole 2x2x4 slice. The times are simulated.
32 devices in a mesh: clip: 8 (over y, x, core), feat: 4 (over z).
Axes of the slice: x: 2, y: 2, z: 4, core: 2. Of those that a mesh axis runs over, the one named last changes fastest.
Arguments:
- features: float32 [6144, 22528], P('clip', 'feat'), may hold values from -20 to 20
- weights: float32 [400, 22528], P(None, 'feat'), may hold values from -0.02665009 to 0.02665009
- labels: int32 [6144], P('clip'), may hold values from 0 to 399
Outputs:
- new_weights: float32 [400, 22528], P(None, 'feat')
- residual: float32 [400, 22528], P(None, 'feat')
All inputs are finite; a program needn't handle non-finite values.
Results may differ from a plain program's by a relative error of at most 0.0003.
Values sent between devices are 32-bit elements; how exact they have to be, the bound alone decides.
No kernel may reach another device: no remote copies, remote signals or barrier semaphores. Data moves between devices by JAX's collectives and lax.ppermute only.
A program may use at most 128 MiB of HBM per device.

v0:
```python
import jax
import jax.numpy as jnp
from jax import lax
from jax.sharding import PartitionSpec as P

ITERS = 2


damping = 0.01


def contract_rows(left, right):
    return lax.dot_general(
        left,
        right,
        (((0,), (0,)), ((), ())),
        precision=lax.Precision.HIGHEST,
        preferred_element_type=jnp.float32,
    )


def contract_feats(left, right):
    return lax.dot_general(
        left,
        right,
        (((1,), (1,)), ((), ())),
        precision=lax.Precision.HIGHEST,
        preferred_element_type=jnp.float32,
    )


def local(features, weights, labels):
    rows_dev = features.shape[0]
    classes = weights.shape[0]
    total_rows = rows_dev * lax.axis_size("clip")

    def reduce_rows(partial_sum):
        return lax.psum(partial_sum, "feat")

    def backward(row_values):
        return lax.psum(contract_rows(row_values, features) / total_rows, "clip")

    logits = reduce_rows(contract_feats(features, weights))
    probs = jax.nn.softmax(logits, axis=1)
    onehot = (labels[:, None] == jnp.arange(classes, dtype=jnp.int32)[None, :]).astype(jnp.float32)
    gradient = backward(probs - onehot)
    residual = -gradient
    solution = jnp.zeros_like(residual)
    direction = residual
    for iteration in range(ITERS):
        tangent = reduce_rows(contract_feats(features, direction))
        bent = probs * tangent - probs * jnp.sum(probs * tangent, axis=1, keepdims=True)
        image = backward(bent) + damping * direction
        norm_now, curvature, cross_term, image_norm = lax.psum(
            (
                jnp.sum(residual * residual),
                jnp.sum(direction * image),
                jnp.sum(residual * image),
                jnp.sum(image * image),
            ),
            "feat",
        )
        step_size = norm_now / curvature
        norm_next = norm_now - 2.0 * step_size * cross_term + step_size * step_size * image_norm
        solution = solution + step_size * direction
        residual = residual - step_size * image
        direction = residual + norm_next / norm_now * direction
    return (weights + solution, residual)


def solution(mesh):
    in_specs = (P("clip", "feat"), P(None, "feat"), P("clip"))
    out_specs = (P(None, "feat"), P(None, "feat"))
    return jax.shard_map(local, mesh=mesh, in_specs=in_specs, out_specs=out_specs, check_vma=False)
```

profile of v0, /device:TPU:0, one launch (start us, length us, event | category | flops | bytes accessed | tf_op | source)
XLA Modules:
  0.0 835.6 jit_solution(1128874775496606367)
XLA Ops:
  7.2 0.0 copy-start.1
  7.2 0.0 all-reduce.9.cloned.1.call-start
  7.2 28.6 %fusion.25 = f32[768,400]{0,1:T(8,128)} fusion(f32[768,5632]{1,0:T(8,128)} %param.3, f32[400,5632]{1,0:T(8,128)} %param.4), kind=kOutput, calls=%fused_computation.35 | convolution fusion | flops 20761804800 | bytes 27541504 | tf_op jit(solution)/shard_map/dot_general | solution.py:23
  35.8 0.0 all-reduce.9.cloned.1.call-update
  35.8 0.6 all-reduce.11.cloned.1.call-start
  36.4 60.0 %all-reduce.9.cloned.1.call-done = f32[768,400]{0,1:T(8,128)} async-done(((f32[768,400]{0,1:T(8,128)}), f32[768,400]{0,1:T(8,128)}) %all-reduce.9.cloned.1.call-update) | async-done | bytes 1228816 | tf_op jit(solution)/shard_map/psum | solution.py:38
  96.4 1.4 reduce_max.9
  97.8 1.5 fusion.12
  99.3 0.0 copy-done.1
  99.3 28.2 %convolution_multiply_fusion.2 = f32[400,5632]{1,0:T(8,128)} fusion(f32[768,5632]{1,0:T(8,128)} %param.3, s32[768]{0:T(1024)S(1)} %copy-done.1, f32[768,400]{0,1:T(8,128)} %all-reduce.9.cloned.1.call-done, f32[768]{0:T(1024)S(1)} %fusion.12, f32[768]{0:T(1024)S(1)} %reduce_max.9), kind=kOutput, calls=%fused_computation.2 | convolution fusion | flops 20765593600 | bytes 27550720 | tf_op jit(solution)/shard_map/dot_general | solution.py:13
  127.5 0.0 all-reduce.11.cloned.1.call-update
  127.5 0.0 copy-start
  127.5 0.2 all-reduce.13.cloned.1.call-start
  127.8 133.0 %all-reduce.11.cloned.1.call-done = f32[400,5632]{1,0:T(8,128)} async-done(((f32[400,5632]{1,0:T(8,128)}), f32[400,5632]{1,0:T(8,128)}) %all-reduce.11.cloned.1.call-update) | async-done | bytes 9011216 | tf_op jit(solution)/shard_map/psum | solution.py:41
  260.7 28.6 %fusion.2 = f32[768,400]{0,1:T(8,128)} fusion(f32[768,5632]{1,0:T(8,128)} %param.3, f32[400,5632]{1,0:T(8,128)} %all-reduce.11.cloned.1.call-done), kind=kOutput, calls=%fused_computation.16 | convolution fusion | flops 20764057600 | bytes 27541504 | tf_op jit(solution)/shard_map/dot_general | solution.py:23
  289.3 0.0 all-reduce.13.cloned.1.call-update
  289.4 0.0 all-reduce.15.cloned.1.call-start
  289.4 57.9 %all-reduce.13.cloned.1.call-done = f32[768,400]{0,1:T(8,128)} async-done(((f32[768,400]{0,1:T(8,128)}), f32[768,400]{0,1:T(8,128)}) %all-reduce.13.cloned.1.call-update) | async-done | bytes 1228816 | tf_op jit(solution)/shard_map/psum | solution.py:38
  347.3 0.0 copy-done
  347.3 1.6 fusion.22
  348.8 28.5 %convolution_multiply_fusion.1 = f32[400,5632]{1,0:T(8,128)} fusion(f32[768,5632]{1,0:T(8,128)} %param.3, f32[768]{0:T(1024)S(1)} %fusion.22, f32[768,400]{0,1:T(8,128)S(1)} %copy-done, f32[768]{0:T(1024)S(1)} %fusion.12, f32[768]{0:T(1024)S(1)} %reduce_max.9, f32[768,400]{0,1:T(8,128)} %all-reduce.13.cloned.1.call-done), kind=kOutput, calls=%fused_computation.1 | convolution fusion | flops 20765593600 | bytes 28779520 | tf_op jit(solution)/shard_map/dot_general | solution.py:13
  377.3 0.0 all-reduce.15.cloned.1.call-update
  377.3 0.3 all-reduce.17.cloned.1.call-start
  377.6 132.9 %all-reduce.15.cloned.1.call-done = f32[400,5632]{1,0:T(8,128)} async-done(((f32[400,5632]{1,0:T(8,128)}), f32[400,5632]{1,0:T(8,128)}) %all-reduce.15.cloned.1.call-update) | async-done | bytes 9011216 | tf_op jit(solution)/shard_map/psum | solution.py:41
  510.5 8.2 multiply_reduce_fusion.1
  518.7 12.3 %all-reduce.1 = (f32[]{:T(128)}, f32[]{:T(128)}, f32[]{:T(128)}) all-reduce(f32[]{:T(128)} %get-tuple-element.6, f32[]{:T(128)} %get-tuple-element.5, f32[]{:T(128)} %get-tuple-element.4), channel_id=1, replica_groups=mesh['clip'=8,'feat'=4] {'feat'}, use_global_device_ids=true, to_apply=%region_5.0 | all-reduce | flops 3 | bytes 24 | tf_op jit(solution)/shard_map/psum | solution.py:54
  534.9 30.6 %convolution_bitcast_fusion = f32[768,400]{0,1:T(8,128)} fusion(f32[768,5632]{1,0:T(8,128)} %param.3, f32[400,5632]{1,0:T(8,128)} %all-reduce.11.cloned.1.call-done, f32[]{:T(128)S(6)} %div.31, f32[400,5632]{1,0:T(8,128)} %all-reduce.15.cloned.1.call-done, f32[]{:T(128)S(6)} %div.30), kind=kOutput, calls=%fused_computation.17 | convolution fusion | flops 20777574400 | bytes 36552712 | tf_op jit(solution)/shard_map/dot_general | solution.py:23
  565.5 0.0 all-reduce.17.cloned.1.call-update
  565.5 0.4 all-reduce.19.cloned.1.call-start
  566.0 54.7 %all-reduce.17.cloned.1.call-done = f32[768,400]{0,1:T(8,128)} async-done(((f32[768,400]{0,1:T(8,128)}), f32[768,400]{0,1:T(8,128)}) %all-reduce.17.cloned.1.call-update) | async-done | bytes 1228816 | tf_op jit(solution)/shard_map/psum | solution.py:38
  620.7 1.5 fusion.24
  622.2 28.5 %convolution_multiply_fusion = f32[400,5632]{1,0:T(8,128)} fusion(f32[768,5632]{1,0:T(8,128)} %param.3, f32[768]{0:T(1024)S(1)} %fusion.24, f32[768,400]{0,1:T(8,128)S(1)} %copy-done, f32[768]{0:T(1024)S(1)} %fusion.12, f32[768]{0:T(1024)S(1)} %reduce_max.9, f32[768,400]{0,1:T(8,128)} %all-reduce.17.cloned.1.call-done), kind=kOutput, calls=%fused_computation | convolution fusion | flops 20765593600 | bytes 28779520 | tf_op jit(solution)/shard_map/dot_general | solution.py:13
  650.7 0.0 all-reduce.19.cloned.1.call-update
  650.7 133.2 %all-reduce.19.cloned.1.call-done = f32[400,5632]{1,0:T(8,128)} async-done(((f32[400,5632]{1,0:T(8,128)}), f32[400,5632]{1,0:T(8,128)}) %all-reduce.19.cloned.1.call-update) | async-done | bytes 9011216 | tf_op jit(solution)/shard_map/psum | solution.py:41
  783.9 11.4 %multiply_reduce_fusion = (f32[]{:T(128)}, f32[]{:T(128)}) fusion(f32[400,5632]{1,0:T(8,128)} %all-reduce.19.cloned.1.call-done, f32[400,5632]{1,0:T(8,128)} %all-reduce.11.cloned.1.call-done, f32[]{:T(128)S(6)} %div.31, f32[400,5632]{1,0:T(8,128)} %all-reduce.15.cloned.1.call-done, f32[]{:T(128)S(6)} %div.30), kind=kLoop, calls=%fused_computation.5 | loop fusion | flops 29286400 | bytes 27033616 | tf_op jit(solution)/shard_map/reduce_sum | solution.py:57
  795.3 12.3 %all-reduce = (f32[]{:T(128)}, f32[]{:T(128)}) all-reduce(f32[]{:T(128)} %get-tuple-element.3, f32[]{:T(128)} %get-tuple-element.2), channel_id=1, replica_groups=mesh['clip'=8,'feat'=4] {'feat'}, use_global_device_ids=true, to_apply=%region_12.0 | all-reduce | flops 2 | bytes 16 | tf_op jit(solution)/shard_map/psum | solution.py:54
  809.0 19.6 %multiply_subtract_fusion = (f32[400,5632]{1,0:T(8,128)}, f32[400,5632]{1,0:T(8,128)}) fusion(f32[400,5632]{1,0:T(8,128)} %all-reduce.19.cloned.1.call-done, f32[]{:T(128)S(6)} %div.33, f32[400,5632]{1,0:T(8,128)} %all-reduce.11.cloned.1.call-done, f32[]{:T(128)S(6)} %div.31, f32[400,5632]{1,0:T(8,128)} %all-reduce.15.cloned.1.call-done, f32[]{:T(128)S(6)} %div.30, ...), kind=kLoop, calls=%fused_computation.3 | loop fusion | flops 33792000 | bytes 54067212 | tf_op jit(solution)/shard_map/sub | solution.py:66
Async XLA Ops:
  7.2 92.1 %copy-start.1 = (s32[768]{0:T(1024)S(1)}, s32[768]{0:T(1024)}, u32[]{:S(2)}) copy-start(s32[768]{0:T(1024)} %param.5) | copy-start | bytes 9220
  7.2 89.2 %all-reduce.9.cloned.1.call-start = ((), (), s32[]{:S(2)}) async-start(), calls=%async_computation | async-start | bytes 2457600 | tf_op jit(solution)/shard_map/psum | solution.py:38
  35.8 224.9 %all-reduce.11.cloned.1.call-start = ((), (), s32[]{:S(2)}) async-start(), calls=%async_computation.1 | async-start | bytes 18022400 | tf_op jit(solution)/shard_map/psum | solution.py:41
  127.5 219.8 %copy-start = (f32[768,400]{0,1:T(8,128)S(1)}, f32[768,400]{0,1:T(8,128)}, u32[]{:S(2)}) copy-start(f32[768,400]{0,1:T(8,128)} %all-reduce.9.cloned.1.call-done) | copy-start | bytes 3686404
  127.5 219.7 %all-reduce.13.cloned.1.call-start = ((), (), s32[]{:S(2)}) async-start(), calls=%async_computation.2 | async-start | bytes 2457600 | tf_op jit(solution)/shard_map/psum | solution.py:38
  289.4 221.1 %all-reduce.15.cloned.1.call-start = ((), (), s32[]{:S(2)}) async-start(), calls=%async_computation.3 | async-start | bytes 18022400 | tf_op jit(solution)/shard_map/psum | solution.py:41
  377.3 243.4 %all-reduce.17.cloned.1.call-start = ((), (), s32[]{:S(2)}) async-start(), calls=%async_computation.4 | async-start | bytes 2457600 | tf_op jit(solution)/shard_map/psum | solution.py:38
  565.5 218.4 %all-reduce.19.cloned.1.call-start = ((), (), s32[]{:S(2)}) async-start(), calls=%async_computation.5 | async-start | bytes 18022400 | tf_op jit(solution)/shard_map/psum | solution.py:41
Sparse Core Ops, SparseCore 0:
  35.9 60.4 all-reduce.8
  127.6 133.0 all-reduce.10
  289.5 57.7 all-reduce.12
  377.4 133.0 all-reduce.14
  565.6 54.9 all-reduce.16
  650.8 133.0 all-reduce.18
where the time goes:
time: 840 us; the launch traced here: 836 us
  waiting for transfers between devices  572 us (68%)
  matrix products  173 us (21%)
  other arithmetic  45.2 us (5%)
  blocking collectives  24.6 us (3%)
  between operations  19.6 us (2%)
    psum x3, waiting for transfers between devices, backward(): return lax.psum(contract_rows(row_values, features) / total_rows, 'clip')  399 us
    psum x3, waiting for transfers between devices, reduce_rows(): return lax.psum(partial_sum, 'feat')  173 us
    dot_general x3, matrix products, contract_feats(): lax.dot_general(left, right, (((1,), (1,)), ((), ())), precision=lax.Prec...  87.8 us
    dot_general x3, matrix products, contract_rows(): lax.dot_general(left, right, (((0,), (0,)), ((), ())), precision=lax.Prec...  85.1 us
    psum x2, blocking collectives, local(): lax.psum((jnp.sum(residual * residual), jnp.sum(direction * image), jnp.s...  24.6 us
    sub x1, other arithmetic, local(): residual = residual - step_size * image  19.6 us
  transfers between devices with their start and end apart: 6, of which 6 were waited for; matrix products, arithmetic and copies ran while one was open for 0% of the time, Pallas kernels for 0%

commit v1 on v0

v1 whole, which is shorter than its diff:
```python
import jax
import jax.numpy as jnp
from jax import lax
from jax.sharding import PartitionSpec as P

damping = 0.01
HIGH = lax.Precision.HIGH


def chunks_of(classes, parts):
    eighths = classes // 8
    starts = [8 * (eighths * k // parts) for k in range(parts)] + [classes]
    return list(zip(starts[:-1], starts[1:]))


def back(row_values, features):
    return lax.dot_general(
        row_values, features, (((1,), (0,)), ((), ())), precision=HIGH, preferred_element_type=jnp.float32
    )


def forth(vectors, features):
    return lax.dot_general(
        vectors, features, (((1,), (1,)), ((), ())), precision=HIGH, preferred_element_type=jnp.float32
    )


def local(features, weights, labels):
    rows = features.shape[0]
    classes = weights.shape[0]
    n_clip, n_feat = lax.axis_size("clip"), lax.axis_size("feat")
    total_rows = rows * n_clip
    ranges = chunks_of(classes, 2)

    def sum_feat(x):
        return lax.psum(x, "feat")

    def sum_clip(x):
        return lax.psum(x, "clip")

    def backward(row_values):
        return [sum_clip(back(row_values[a:b], features)) for a, b in ranges]

    def forward(vectors):
        return [sum_feat(forth(v, features)) for v in vectors]

    def bend(probs, tangent):
        weighted = probs * tangent
        return (weighted - probs * jnp.sum(weighted, axis=0, keepdims=True)) / total_rows

    logits = sum_feat(forth(weights, features))
    top = jnp.max(logits, axis=0, keepdims=True)
    powers = jnp.exp(logits - top)
    probs = powers / jnp.sum(powers, axis=0, keepdims=True)
    onehot = (labels[None, :] == jnp.arange(classes, dtype=jnp.int32)[:, None]).astype(jnp.float32)

    direction = [-g for g in backward((probs - onehot) / total_rows)]
    tangent = jnp.concatenate(forward(direction), axis=0)
    bent = bend(probs, tangent)
    norm = sum(jnp.sum(d * d) for d in direction)
    both = lax.psum(jnp.stack([norm / n_clip, jnp.sum(bent * tangent) / n_feat]), ("clip", "feat"))
    norm0, curvature0 = both[0], both[1] + damping * both[0]
    step0 = norm0 / curvature0

    image = backward(bent)
    residual = [d - step0 * (i + damping * d) for d, i in zip(direction, image)]
    inner = jnp.stack([
        sum(jnp.sum(r * r) for r in residual),
        sum(jnp.sum(r * d) for r, d in zip(residual, direction)),
    ])
    inner = lax.psum(inner, "feat")
    norm1 = inner[0]
    ratio = norm1 / norm0
    tangent = jnp.concatenate(forward(residual), axis=0) + ratio * tangent
    bent = bend(probs, tangent)
    length = norm1 + 2.0 * ratio * inner[1] + ratio * ratio * norm0
    curvature1 = lax.psum(jnp.sum(bent * tangent), "clip") + damping * length
    step1 = norm1 / curvature1

    image = backward(bent)
    following = [r + ratio * d for r, d in zip(residual, direction)]
    moved = [step0 * d + step1 * f for d, f in zip(direction, following)]
    last = [r - step1 * (i + damping * f) for r, i, f in zip(residual, image, following)]
    return weights + jnp.concatenate(moved, axis=0), jnp.concatenate(last, axis=0)


def solution(mesh):
    in_specs = (P("clip", "feat"), P(None, "feat"), P("clip"))
    out_specs = (P(None, "feat"), P(None, "feat"))
    return jax.shard_map(local, mesh=mesh, in_specs=in_specs, out_specs=out_specs, check_vma=False)
```

time: 840 us -> 798 us (0.950)
  waiting for transfers between devices: 572 us -> 477 us
  blocking collectives: 24.6 us -> 68.3 us
  other arithmetic: 45.2 us -> 59.4 us
  matrix products: 173 us -> 163 us
    psum x6, waiting for transfers between devices: 572 us -> 477 us  [the longest x3 329 us: sum_clip(): return lax.psum(x, 'clip')]
    psum x2 -> x3, blocking collectives: 24.6 us -> 68.3 us  [the longest x1 40.9 us: local(): lax.psum(jnp.stack([norm / n_clip, jnp.sum(bent * tangent) / n_feat]), ('...]
    dot_general x6 -> x11, matrix products: 173 us -> 163 us  [the longest x5 91.4 us: forth(): lax.dot_general(vectors, features, (((1,), (1,)), ((), ())), precision=HI...]
    reduce_sum x5 -> x9, other arithmetic: 24.2 us -> 27.1 us  [the longest x2 11.3 us: local(): jnp.sum(r * r)]
  transfers between devices with their start and end apart: 6 -> 6, of which waited for: 6 -> 6; matrix products, arithmetic and copies ran while one was open for 0% -> 3% of each run, Pallas kernels for 0% -> 0%
where the time goes in v1:
time: 798 us
  waiting for transfers between devices  477 us (60%)
  matrix products  163 us (20%)
  blocking collectives  68.3 us (9%)
  other arithmetic  59.4 us (7%)
  between operations  25 us (3%)
    psum x3, waiting for transfers between devices, sum_clip(): return lax.psum(x, 'clip')  329 us
    psum x3, waiting for transfers between devices, sum_feat(): return lax.psum(x, 'feat')  148 us
    dot_general x5, matrix products, forth(): lax.dot_general(vectors, features, (((1,), (1,)), ((), ())), precision=HI...  91.4 us
    dot_general x6, matrix products, back(): lax.dot_general(row_values, features, (((1,), (0,)), ((), ())), precision...  71.6 us
    psum x1, blocking collectives, local(): lax.psum(jnp.stack([norm / n_clip, jnp.sum(bent * tangent) / n_feat]), ('...  40.9 us
  transfers between devices with their start and end apart: 6, of which 6 were waited for; matrix products, arithmetic and copies ran while one was open for 3% of the time, Pallas kernels for 0%

profile of v1, /device:TPU:0, one launch (start us, length us, event | category | flops | bytes accessed | tf_op | source)
XLA Modules:
  0.0 797.7 jit_solution(5066950116147351699)
XLA Ops:
  7.2 0.0 copy-start.3
  7.2 0.0 all-reduce.12.cloned.1.call-start
  7.2 17.4 %fusion.26 = f32[400,768]{1,0:T(8,128)} fusion(f32[400,5632]{1,0:T(8,128)} %param.4, f32[768,5632]{1,0:T(8,128)} %param.3), kind=kOutput, calls=%fused_computation.54 | convolution fusion | flops 10380902400 | bytes 27541504 | tf_op jit(solution)/shard_map/dot_general | solution.py:23
  24.6 0.0 all-reduce.12.cloned.1.call-update
  24.6 0.5 all-reduce.18.cloned.1.call-start
  25.1 60.1 %all-reduce.12.cloned.1.call-done = f32[400,768]{1,0:T(8,128)} async-done(((f32[400,768]{1,0:T(8,128)}), f32[400,768]{1,0:T(8,128)}) %all-reduce.12.cloned.1.call-update) | async-done | bytes 1228816 | tf_op jit(solution)/shard_map/psum | solution.py:36
  85.2 1.4 reduce_max.9
  86.6 1.5 fusion.5
  88.1 0.0 copy-done.3
  88.1 1.6 subtract_multiply_fusion.2
  89.7 0.0 copy-start
  89.7 14.2 %fusion.14 = f32[200,5632]{1,0:T(8,128)} fusion(f32[768,5632]{1,0:T(8,128)} %param.3, f32[400,768]{1,0:T(8,128)S(1)} %subtract_multiply_fusion.2), kind=kOutput, calls=%fused_computation.38 | convolution fusion | flops 5190451200 | bytes 22421504 | tf_op jit(solution)/shard_map/dot_general | solution.py:17
  103.9 0.0 copy-done
  103.9 8.7 %fusion.16 = f32[200,5632]{1,0:T(8,128)} fusion(f32[768,5632]{1,0:T(8,128)S(1)} %copy-done, f32[400,768]{1,0:T(8,128)S(1)} %subtract_multiply_fusion.2), kind=kOutput, calls=%fused_computation.40 | convolution fusion | flops 5190451200 | bytes 22421504 | tf_op jit(solution)/shard_map/dot_general | solution.py:17
  112.5 0.0 all-reduce.18.cloned.1.call-update
  112.6 0.2 all-reduce.22.cloned.1.call-start
  112.8 133.3 %all-reduce.18.cloned.1.call-done = (f32[200,5632]{1,0:T(8,128)}, f32[200,5632]{1,0:T(8,128)}) async-done(((f32[200,5632]{1,0:T(8,128)}, f32[200,5632]{1,0:T(8,128)}), (f32[200,5632]{1,0:T(8,128)}, f32[200,5632]{1,0:T(8,128)})) %all-reduce.18.cloned.1.call-update) | async-done | bytes 9011216 | tf_op jit(solution)/shard_map/psum | solution.py:39
  246.1 0.0 copy-start.1
  246.1 14.0 %fusion = f32[200,768]{1,0:T(8,128)} fusion(f32[768,5632]{1,0:T(8,128)} %param.3, f32[200,5632]{1,0:T(8,128)} %get-tuple-element.10), kind=kOutput, calls=%fused_computation.16 | convolution fusion | flops 5191577600 | bytes 22421504 | tf_op jit(solution)/shard_map/dot_general | solution.py:23
  260.1 0.0 copy-done.1
  260.1 13.2 %fusion.2 = f32[200,768]{1,0:T(8,128)} fusion(f32[768,5632]{1,0:T(8,128)} %param.3, f32[200,5632]{1,0:T(8,128)S(1)} %copy-done.1), kind=kOutput, calls=%fused_computation.18 | convolution fusion | flops 5191577600 | bytes 22421504 | tf_op jit(solution)/shard_map/dot_general | solution.py:23
  273.4 0.0 copy-start.2
  273.4 0.0 all-reduce.22.cloned.1.call-update
  273.4 0.3 all-reduce.16.cloned.1.call-start
  273.7 58.0 %all-reduce.22.cloned.1.call-done = (f32[200,768]{1,0:T(8,128)}, f32[200,768]{1,0:T(8,128)}) async-done(((f32[200,768]{1,0:T(8,128)}, f32[200,768]{1,0:T(8,128)}), (f32[200,768]{1,0:T(8,128)}, f32[200,768]{1,0:T(8,128)})) %all-reduce.22.cloned.1.call-update) | async-done | bytes 1228816 | tf_op jit(solution)/shard_map/psum | solution.py:36
  331.6 1.1 constant_dynamic-update-slice_fusion.1
  332.8 1.1 constant_dynamic-update-slice_fusion
  333.9 0.0 copy-done.2
  333.9 0.3 fusion.21
  334.2 1.1 multiply_reduce_fusion.7
  335.2 12.2 %fusion.12 = f32[200,5632]{1,0:T(8,128)} fusion(f32[768,5632]{1,0:T(8,128)} %param.3, f32[400,768]{1,0:T(8,128)S(1)} %get-tuple-element.19), kind=kOutput, calls=%fused_computation.36 | convolution fusion | flops 5190451200 | bytes 22421504 | tf_op jit(solution)/shard_map/dot_general | solution.py:17
  347.4 12.2 %fusion.10 = f32[200,5632]{1,0:T(8,128)} fusion(f32[768,5632]{1,0:T(8,128)} %param.3, f32[400,768]{1,0:T(8,128)S(1)} %get-tuple-element.19), kind=kOutput, calls=%fused_computation.34 | convolution fusion | flops 5190451200 | bytes 22421504 | tf_op jit(solution)/shard_map/dot_general | solution.py:17
  359.6 0.0 all-reduce.16.cloned.1.call-update
  359.7 0.0 all-reduce.20.cloned.1.call-start
  359.7 4.0 multiply_reduce_fusion.5
  363.8 0.0 slice-start
  363.8 5.0 multiply_reduce_fusion.4
  370.8 0.1 pad_maximum_fusion.1
  370.8 40.9 %psum.103 = f32[2]{0:T(128)S(1)} all-reduce(f32[2]{0:T(128)S(1)} %pad_maximum_fusion.1), channel_id=1, replica_groups=mesh['clip'=8,'feat'=4] {'clip','feat'}, use_global_device_ids=true, to_apply=%region_11.0 | all-reduce | flops 2 | bytes 16 | tf_op jit(solution)/shard_map/psum | solution.py:61
  411.7 0.7 fusion.25
  414.2 79.9 %all-reduce.16.cloned.1.call-done = (f32[200,5632]{1,0:T(8,128)}, f32[200,5632]{1,0:T(8,128)}) async-done(((f32[200,5632]{1,0:T(8,128)}, f32[200,5632]{1,0:T(8,128)}), (f32[200,5632]{1,0:T(8,128)}, f32[200,5632]{1,0:T(8,128)})) %all-reduce.16.cloned.1.call-update) | async-done | bytes 9011216 | tf_op jit(solution)/shard_map/psum | solution.py:39
  494.1 0.0 slice-start.1
  494.1 18.5 %fusion.22 = f32[200,768]{1,0:T(8,128)} fusion(f32[768,5632]{1,0:T(8,128)} %param.3, f32[200,5632]{1,0:T(8,128)} %get-tuple-element.8, f32[200,5632]{1,0:T(8,128)} %get-tuple-element.11, f32[]{:T(128)S(6)} %div.38), kind=kOutput, calls=%fused_computation.50 | convolution fusion | flops 5196083200 | bytes 26927108 | tf_op jit(solution)/shard_map/dot_general | solution.py:23
  512.6 0.0 slice-done
  512.6 0.0 slice-done.1
  512.6 28.3 %fusion.23 = f32[200,768]{1,0:T(8,128)} fusion(f32[768,5632]{1,0:T(8,128)} %param.3, f32[200,5632]{1,0:T(8,128)} %get-tuple-element.9, f32[200,5632]{1,0:T(8,128)S(1)} %bitcast.21, f32[]{:T(128)S(6)} %div.38), kind=kOutput, calls=%fused_computation.51 | convolution fusion | flops 5196083200 | bytes 26927108 | tf_op jit(solution)/shard_map/dot_general | solution.py:23
  540.9 0.0 all-reduce.20.cloned.1.call-update
  540.9 0.0 all-reduce.14.cloned.1.call-start
  541.0 5.6 multiply_reduce_fusion.3
  546.6 5.6 multiply_reduce_fusion.2
  554.8 0.1 pad_maximum_fusion.2
  554.9 12.4 %psum.106 = f32[2]{0:T(128)S(1)} all-reduce(f32[2]{0:T(128)S(1)} %pad_maximum_fusion.2), channel_id=1, replica_groups=mesh['clip'=8,'feat'=4] {'feat'}, use_global_device_ids=true, to_apply=%region_18.0 | all-reduce | flops 2 | bytes 16 | tf_op jit(solution)/shard_map/psum | solution.py:71
  567.3 0.6 fusion.24
  569.1 30.3 %all-reduce.20.cloned.1.call-done = (f32[200,768]{1,0:T(8,128)}, f32[200,768]{1,0:T(8,128)}) async-done(((f32[200,768]{1,0:T(8,128)}, f32[200,768]{1,0:T(8,128)}), (f32[200,768]{1,0:T(8,128)}, f32[200,768]{1,0:T(8,128)})) %all-reduce.20.cloned.1.call-update) | async-done | bytes 1228816 | tf_op jit(solution)/shard_map/psum | solution.py:36
  599.4 1.6 fusion.19
  601.0 2.3 multiply_reduce_fusion.6
  603.4 12.2 %fusion.8 = f32[200,5632]{1,0:T(8,128)} fusion(f32[768,5632]{1,0:T(8,128)} %param.3, f32[400,768]{1,0:T(8,128)S(1)} %get-tuple-element.17), kind=kOutput, calls=%fused_computation.32 | convolution fusion | flops 5190451200 | bytes 22421504 | tf_op jit(solution)/shard_map/dot_general | solution.py:17
  615.6 12.2 %fusion.6 = f32[200,5632]{1,0:T(8,128)} fusion(f32[768,5632]{1,0:T(8,128)} %param.3, f32[400,768]{1,0:T(8,128)S(1)} %get-tuple-element.17), kind=kOutput, calls=%fused_computation.30 | convolution fusion | flops 5190451200 | bytes 22421504 | tf_op jit(solution)/shard_map/dot_general | solution.py:17
  627.8 0.0 all-reduce.14.cloned.1.call-update
  629.6 15.1 %psum.109 = f32[]{:T(128)} all-reduce(f32[]{:T(128)} %get-tuple-element.16), channel_id=1, replica_groups=mesh['clip'=8,'feat'=4] {'clip'}, use_global_device_ids=true, to_apply=%region_23.0 | all-reduce | flops 1 | bytes 8 | tf_op jit(solution)/shard_map/psum | solution.py:77
  645.9 115.7 %all-reduce.14.cloned.1.call-done = (f32[200,5632]{1,0:T(8,128)}, f32[200,5632]{1,0:T(8,128)}) async-done(((f32[200,5632]{1,0:T(8,128)}, f32[200,5632]{1,0:T(8,128)}), (f32[200,5632]{1,0:T(8,128)}, f32[200,5632]{1,0:T(8,128)})) %all-reduce.14.cloned.1.call-update) | async-done | bytes 9011216 | tf_op jit(solution)/shard_map/psum | solution.py:39
  761.6 14.6 %multiply_subtract_fusion = (f32[200,5632]{1,0:T(8,128)}, f32[200,5632]{1,0:T(8,128)S(1)}, f32[200,5632]{1,0:T(8,128)S(1)}, f32[200,5632]{1,0:T(8,128)}) fusion(f32[200,5632]{1,0:T(8,128)} %get-tuple-element.6, f32[200,5632]{1,0:T(8,128)} %get-tuple-element.10, f32[]{:T(128)S(6)} %div.39, f32[]{:T(128)S(6)} %div.41, f32[200,5632]{1,0:T(8,128)} %get-tuple-element.9, ...), kind=kLoop, calls=%fused_computation.2 | loop fusion | flops 31539200 | bytes 45056012 | tf_op jit(solution)/shard_map/sub | solution.py:83
  776.2 7.9 pad_maximum_fusion
  784.0 6.6 maximum_add_fusion
  (1 shorter events, 0.0 us)
Async XLA Ops:
  7.2 80.9 %copy-start.3 = (s32[768]{0:T(1024)S(1)}, s32[768]{0:T(1024)}, u32[]{:S(2)}) copy-start(s32[768]{0:T(1024)} %param.5) | copy-start | bytes 9220
  7.2 78.0 %all-reduce.12.cloned.1.call-start = ((), (), s32[]{:S(2)}) async-start(), calls=%async_computation | async-start | bytes 2457600 | tf_op jit(solution)/shard_map/psum | solution.py:36
  24.6 221.5 %all-reduce.18.cloned.1.call-start = ((), (), s32[]{:S(2)}) async-start(), calls=%async_computation.3 | async-start | bytes 18022400 | tf_op jit(solution)/shard_map/psum | solution.py:39
  89.7 14.2 %copy-start = (f32[768,5632]{1,0:T(8,128)S(1)}, f32[768,5632]{1,0:T(8,128)}, u32[]{:S(2)}) copy-start(f32[768,5632]{1,0:T(8,128)} %param.3) | copy-start | bytes 51904516
  112.6 219.1 %all-reduce.22.cloned.1.call-start = ((), (), s32[]{:S(2)}) async-start(), calls=%async_computation.5 | async-start | bytes 2457600 | tf_op jit(solution)/shard_map/psum | solution.py:36
  246.1 14.0 %copy-start.1 = (f32[200,5632]{1,0:T(8,128)S(1)}, f32[200,5632]{1,0:T(8,128)}, u32[]{:S(2)}) copy-start(f32[200,5632]{1,0:T(8,128)} %get-tuple-element.11) | copy-start | bytes 13516804
  273.4 60.5 %copy-start.2 = (f32[400,768]{1,0:T(8,128)S(1)}, f32[400,768]{1,0:T(8,128)}, u32[]{:S(2)}) copy-start(f32[400,768]{1,0:T(8,128)} %all-reduce.12.cloned.1.call-done) | copy-start | bytes 3686404
  273.4 220.7 %all-reduce.16.cloned.1.call-start = ((), (), s32[]{:S(2)}) async-start(), calls=%async_computation.2 | async-start | bytes 18022400 | tf_op jit(solution)/shard_map/psum | solution.py:39
  359.7 239.8 %all-reduce.20.cloned.1.call-start = ((), (), s32[]{:S(2)}) async-start(), calls=%async_computation.4 | async-start | bytes 2457600 | tf_op jit(solution)/shard_map/psum | solution.py:36
  363.8 148.8 %slice-start = ((s8[4505600]{0:T(1024)(128)(4,1)}), s8[311296]{0:T(1024)(128)(4,1)S(1)}, s32[]{:S(2)}) async-start(s8[4505600]{0:T(1024)(128)(4,1)} %bitcast.20), calls=%async_computation.6 | async-start | bytes 622592
  494.1 18.5 %slice-start.1 = ((s8[4505600]{0:T(1024)(128)(4,1)}), s8[4194304]{0:T(1024)(128)(4,1)S(1)}, s32[]{:S(2)}) async-start(s8[4505600]{0:T(1024)(128)(4,1)} %bitcast.20), calls=%async_computation.7 | async-start | bytes 8388608
  540.9 220.7 %all-reduce.14.cloned.1.call-start = ((), (), s32[]{:S(2)}) async-start(), calls=%async_computation.1 | async-start | bytes 18022400 | tf_op jit(solution)/shard_map/psum | solution.py:39
Sparse Core Ops, SparseCore 0:
  24.7 60.4 all-reduce.11
  112.7 133.3 all-reduce.17
  273.5 58.0 all-reduce.21
  359.8 134.2 all-reduce.15
  541.0 58.3 all-reduce.19
  627.9 133.5 all-reduce.13
